TPU v7x, 512 devices: a whole 4x4x16 slice. The times are simulated.
512 devices in a mesh: chan: 32 (over z, y_lo), row: 2 (over core), col: 8 (over x, y_hi).
Axes of the slice: x: 4, y: 4 (y_hi: 2, y_lo: 2; y = y_hi * 2 + y_lo), z: 16, core: 2. Of those that a mesh axis runs over, the one named last changes fastest.
Arguments:
- volts: bfloat16 [2, 1024, 2, 52736], P(None, ('chan', 'row', 'col')), may hold values from -6 to 6
- taps: float32 [8, 512], replicated, may hold values from -2 to 2
- owner_map: int32 [384], replicated, may hold values from 0 to 255, as said below
- assign: int32 [512], replicated, may hold values from 0 to 511, each once
Outputs:
- visibility: bfloat16 [512, 2, 1024, 1024], P(('chan', 'col'), None, 'row')
Inputs may be any that keep to these rules, and one draw needn't show every extreme that they name: `owner_map`: each owner holds 1 to 2 channels, and some owner holds exactly 2. `assign`: A permutation of the stations.
All inputs are finite; a program needn't handle non-finite values.
Results may differ from a plain program's by a relative error of at most 0.0055.
Values may be sent and summed in bfloat16 or wider, within the bound.
A program may use at most 64 MiB of HBM per device.

v0:
```python
import math
import jax
import jax.numpy as jnp
from jax import lax
from jax.sharding import PartitionSpec as P

STATIONS = 512
NFFT = 512
TAPS = 8
BATCHES = 2
CAP = 2


def slot_table(owner_map, owner_count, slot_count):
    channel_count = owner_map.shape[0]
    ranking = jnp.argsort(owner_map * channel_count + jnp.arange(channel_count, dtype=jnp.int32))
    counts = jnp.sum(
        (owner_map[None, :] == jnp.arange(owner_count, dtype=jnp.int32)[:, None]).astype(jnp.int32),
        axis=1,
    )
    starts = jnp.cumsum(counts) - counts
    slot_index = jnp.arange(slot_count, dtype=jnp.int32)
    position = jnp.clip(starts[:, None] + slot_index[None, :], 0, channel_count - 1)
    channel = jnp.take(ranking, position, axis=0)
    is_live = slot_index[None, :] < counts[:, None]
    return (channel, is_live)


def shards(volts, taps, owner_map, assign):
    chan_count = lax.axis_size("chan")
    rows_count = lax.axis_size("row")
    cols_count = lax.axis_size("col")
    owner_count = chan_count * cols_count
    local_inputs = volts.shape[1]
    spec_len = volts.shape[3] // NFFT - TAPS + 1
    channel, is_live = slot_table(owner_map, owner_count, CAP)
    points = jnp.arange(NFFT, dtype=jnp.int32)
    phase = (points[:, None, None] * channel.T[None, :, :] % NFFT).astype(jnp.float32) * (
        2.0 * math.pi / NFFT
    )
    weight_live = is_live.T[None, :, :].astype(jnp.float32) / math.sqrt(NFFT)
    cosine = jnp.cos(phase) * weight_live
    sine = jnp.sin(phase) * weight_live
    table = jnp.stack(
        [jnp.stack([cosine, -sine], axis=1), jnp.stack([sine, cosine], axis=1)], axis=0
    )
    total_inputs = 2 * STATIONS
    positions = jnp.arange(total_inputs, dtype=jnp.int32)
    pick = 2 * jnp.take(assign, positions // 2, axis=0) + positions % 2
    device_of = pick // local_inputs
    within = pick % local_inputs
    chan_of = device_of // (rows_count * cols_count)
    row_of = device_of // cols_count % rows_count
    col_of = device_of % cols_count
    located = ((row_of * cols_count + col_of) * chan_count + chan_of) * local_inputs + within
    row_count = total_inputs // rows_count
    row_pick = lax.dynamic_slice_in_dim(located, lax.axis_index("row") * row_count, row_count)
    total = jnp.zeros((CAP, 2 * row_count, total_inputs), jnp.float32)
    for batch in range(BATCHES):
        signal = (
            volts[batch].astype(jnp.float32).reshape(local_inputs, 2, spec_len + TAPS - 1, NFFT)
        )
        summed = jnp.zeros((local_inputs, 2, spec_len, NFFT), jnp.float32)
        for tap_index in range(TAPS):
            summed = (
                summed
                + taps[tap_index][None, None, None, :]
                * signal[:, :, tap_index : tap_index + spec_len, :]
            )
        result = jnp.einsum("iasj,ajbkg->kgibs", summed, table, precision=lax.Precision.HIGHEST)
        turned = lax.all_to_all(
            lax.all_to_all(
                result.reshape(CAP, chan_count, cols_count, local_inputs, 2 * spec_len).astype(
                    jnp.bfloat16
                ),
                "chan",
                split_axis=1,
                concat_axis=3,
                tiled=True,
            ),
            "col",
            split_axis=2,
            concat_axis=3,
            tiled=True,
        )
        gathered = lax.all_gather(turned, "row", axis=3, tiled=True)
        flat = gathered.reshape(CAP, total_inputs, -1)
        width = flat.shape[2]
        rows = jnp.take(flat, row_pick, axis=1)
        split_rows = rows.reshape(CAP, row_count, width // (2 * spec_len), 2, spec_len)
        flipped = jnp.stack(
            [split_rows[:, :, :, 1, :], -split_rows[:, :, :, 0, :]], axis=3
        ).reshape(CAP, row_count, width)
        stacked = jnp.concatenate([rows, flipped], axis=1)
        columns = jnp.take(flat, located, axis=1)
        total = total + jnp.einsum(
            "kpx,kqx->kpq", stacked, columns, preferred_element_type=jnp.float32
        )
    scale = 1.0 / math.sqrt(2 * BATCHES * spec_len)
    return (total * scale).reshape(CAP, 2, row_count, total_inputs).astype(jnp.bfloat16)


def solution(mesh):
    placed = (P(None, ("chan", "row", "col"), None, None), P(), P(), P())
    return jax.shard_map(
        shards,
        mesh=mesh,
        in_specs=placed,
        out_specs=P(("chan", "col"), None, "row", None),
        check_vma=False,
    )
```

profile of v0, /device:TPU:1, one launch (start us, length us, event | category | flops | bytes accessed | tf_op | source)
XLA Modules:
  0.0 180.4 jit_solution(5233471085927798527)
XLA Ops:
  0.0 0.0 copy-start
  0.0 0.8 convert_reduce_fusion
  0.8 0.7 iota_add_fusion
  1.5 0.3 reduce-window.9
  1.8 0.1 slice.105
  1.9 0.1 slice_reduce_fusion
  2.0 0.1 bitcast_subtract_fusion
  2.1 1.0 fusion.107
  3.2 0.1 compare_select_fusion
  3.3 0.1 reshape.329
  3.4 3.8 %sort.17 = (s32[384]{0:T(512)}, s32[384]{0:T(512)S(1)}) sort(s32[384]{0:T(512)S(1)} %iota_add_fusion, s32[384]{0:T(512)S(1)} %iota.40), dimensions={0}, to_apply=%region_3.4 | sort | flops 3456 | bytes 6144 | tf_op jit(solution)/shard_map/jit(argsort)/sort | solution.py:16
  7.2 0.0 copy-start.3
  7.2 3.5 %gather_fusion = s32[512]{0:T(512)S(1)} fusion(s32[384]{0:T(512)S(1)} %get-tuple-element.8, s32[1024]{0:T(1024)S(1)} %pad_clamp_fusion.1), kind=kCustom, calls=%fused_computation.4 | custom fusion | bytes 6144 | tf_op jit(solution)/shard_map/jit(_take)/gather | solution.py:24
  10.7 0.1 reshape.328
  10.9 0.1 bitcast_select_fusion
  11.0 0.1 copy.54
  11.1 0.0 copy-done.3
  11.1 0.6 slice_convert_fusion
  11.7 1.5 reshape.293
  13.2 4.2 %fusion.71 = (f32[512,1,2,256]{3,0,2,1:T(8,128)S(1)}, f32[512,1,2,256]{3,0,2,1:T(8,128)S(1)}, f32[512,1,2,256]{3,0,2,1:T(8,128)S(1)}) fusion(f32[2,256]{1,0:T(2,128)S(1)} %compare_select_fusion.6, s32[2,256]{1,0:T(2,128)S(1)} %copy.54), kind=kLoop, calls=%fused_computation.100 | loop fusion | flops 4456448 | bytes 3149824 | tf_op jit(solution)/shard_map/neg | solution.py:45
  17.4 0.0 copy-start.2
  17.4 0.3 maximum_bitcast_fusion.3
  17.7 0.0 copy-start.1
  17.7 1.3 copy-done.1
  19.0 0.0 copy-done.2
  19.0 4.6 %fusion.6 = bf16[2,256,2,2,96]{1,4,2,0,3:T(8,128)(2,1)} fusion(f32[1,512,2,2,256]{4,1,0,3,2:T(8,128)S(1)} %get-tuple-element.14, f32[1,512,2,2,256]{4,1,0,3,2:T(8,128)S(1)} %get-tuple-element.13, f32[2,2,103,512]{3,2,1,0:T(8,128)S(1)} %copy-done.2, f32[512]{0:T(512)S(1)} %bitcast.127, f32[512]{0:T(512)S(1)} %bitcast.129, f32[512]{0:T(512)S(1)} %bitcast.117, ...), kind=kOutput, calls=%fused_computation.21 | convolution fusion | flops 2420113408 | bytes 10895360 | tf_op jit(solution)/shard_map/iasj,ajbkg->kgibs/dot_general | solution.py:70
  23.7 1.3 copy.56
  25.0 1.1 convert_element_type.68
  26.1 1.9 %copy.57 = bf16[2,32,8,2,192]{4,2,3,0,1:T(8,128)(2,1)} copy(bf16[2,32,8,2,192]{4,2,1,3,0:T(8,128)(2,1)} %convert_element_type.68) | data formatting | bytes 786432 | tf_op jit(solution)/shard_map/convert_element_type | solution.py:73
  28.0 17.0 %all-to-all-start = ((bf16[2,32,8,2,192]{4,2,3,0,1:T(8,128)(2,1)}), bf16[2,32,8,2,192]{4,2,3,0,1:T(8,128)(2,1)S(1)}, u32[]{:S(2)}, u32[]{:S(2)}) async-start(bf16[2,32,8,2,192]{4,2,3,0,1:T(8,128)(2,1)} %copy.57), calls=%async_computation | async-start | bytes 1048576 | tf_op jit(solution)/shard_map/all_to_all | solution.py:72
  45.1 1.5 reshape.294
  46.6 9.2 %fusion.7 = bf16[2,256,2,2,96]{1,4,2,0,3:T(8,128)(2,1)} fusion(f32[1,512,2,2,256]{4,1,0,3,2:T(8,128)} %copy-done.1, f32[1,512,2,2,256]{4,1,0,3,2:T(8,128)S(1)} %get-tuple-element.13, f32[2,2,103,512]{3,2,1,0:T(8,128)} %reshape.294, f32[512]{0:T(512)S(1)} %bitcast.128, f32[512]{0:T(512)S(1)} %bitcast.130, f32[512]{0:T(512)S(1)} %bitcast.118, ...), kind=kOutput, calls=%fused_computation.22 | convolution fusion | flops 2420113408 | bytes 10895360 | tf_op jit(solution)/shard_map/iasj,ajbkg->kgibs/dot_general | solution.py:70
  55.8 1.3 copy.65
  57.1 0.3 convert_element_type.73
  57.4 0.9 copy.66
  58.3 17.8 %all-to-all-done = bf16[2,32,8,2,192]{4,2,3,0,1:T(8,128)(2,1)S(1)} async-done(((bf16[2,32,8,2,192]{4,2,3,0,1:T(8,128)(2,1)}), bf16[2,32,8,2,192]{4,2,3,0,1:T(8,128)(2,1)S(1)}, u32[]{:S(2)}, u32[]{:S(2)}) %all-to-all-start) | async-done | bytes 393248 | tf_op jit(solution)/shard_map/all_to_all | solution.py:72
  76.0 5.2 %all-to-all-start.2 = ((bf16[2,32,8,2,192]{4,2,3,0,1:T(8,128)(2,1)}), bf16[2,32,8,2,192]{4,2,3,0,1:T(8,128)(2,1)S(1)}, u32[]{:S(2)}, u32[]{:S(2)}) async-start(bf16[2,32,8,2,192]{4,2,3,0,1:T(8,128)(2,1)} %copy.66), calls=%async_computation.2 | async-start | bytes 1048576 | tf_op jit(solution)/shard_map/all_to_all | solution.py:72
  81.3 0.9 copy.59
  82.3 29.5 %all-to-all-done.2 = bf16[2,32,8,2,192]{4,2,3,0,1:T(8,128)(2,1)S(1)} async-done(((bf16[2,32,8,2,192]{4,2,3,0,1:T(8,128)(2,1)}), bf16[2,32,8,2,192]{4,2,3,0,1:T(8,128)(2,1)S(1)}, u32[]{:S(2)}, u32[]{:S(2)}) %all-to-all-start.2) | async-done | bytes 393248 | tf_op jit(solution)/shard_map/all_to_all | solution.py:72
  111.7 6.3 %all-to-all-start.1 = ((bf16[2,1,8,64,192]{4,3,0,1,2:T(8,128)(2,1)}), bf16[2,1,8,64,192]{4,3,0,1,2:T(8,128)(2,1)S(1)}, u32[]{:S(2)}, u32[]{:S(2)}) async-start(bf16[2,1,8,64,192]{4,3,0,1,2:T(8,128)(2,1)} %copy.59), calls=%async_computation.1 | async-start | bytes 1048576 | tf_op jit(solution)/shard_map/all_to_all | solution.py:71
  118.1 0.0 copy-done
  118.1 6.9 %gather_fusion.1 = s32[1024]{0:T(1024)S(1)} fusion(s32[512]{0:T(512)S(1)} %copy-done, s32[1024]{0:T(1024)S(1)} %broadcast_clamp_fusion), kind=kCustom, calls=%fused_computation.5 | custom fusion | bytes 12288 | tf_op jit(solution)/shard_map/jit(_take)/gather | solution.py:49
  125.0 0.9 copy.68
  125.9 0.7 all-to-all-done.1
  126.6 6.0 %all-to-all-start.3 = ((bf16[2,1,8,64,192]{4,3,0,1,2:T(8,128)(2,1)}), bf16[2,1,8,64,192]{4,3,0,1,2:T(8,128)(2,1)S(1)}, u32[]{:S(2)}, u32[]{:S(2)}) async-start(bf16[2,1,8,64,192]{4,3,0,1,2:T(8,128)(2,1)} %copy.68), calls=%async_computation.3 | async-start | bytes 1048576 | tf_op jit(solution)/shard_map/all_to_all | solution.py:71
  132.6 0.1 compare_and_fusion.1
  132.7 0.2 copy.61
  132.9 8.2 %all-to-all-done.3 = bf16[2,1,8,64,192]{4,3,0,1,2:T(8,128)(2,1)S(1)} async-done(((bf16[2,1,8,64,192]{4,3,0,1,2:T(8,128)(2,1)}), bf16[2,1,8,64,192]{4,3,0,1,2:T(8,128)(2,1)S(1)}, u32[]{:S(2)}, u32[]{:S(2)}) %all-to-all-start.3) | async-done | bytes 393248 | tf_op jit(solution)/shard_map/all_to_all | solution.py:71
  141.2 0.2 copy.70
  141.4 7.5 %all_gather.7 = bf16[2,1,1,1024,192]{3,4,2,1,0:T(8,128)(2,1)S(1)} all-gather(bf16[2,1,1,512,192]{3,4,2,1,0:T(8,128)(2,1)S(1)} %copy.70), channel_id=1, replica_groups=mesh['chan'=32,'row'=2,'col'=8] {'row'}, dimensions={3}, use_global_device_ids=true | all-gather | bytes 1179648 | tf_op jit(solution)/shard_map/all_gather | solution.py:86
  148.9 0.9 copy.71
  149.8 2.6 %all_gather.6 = bf16[2,1,1,1024,192]{3,4,2,1,0:T(8,128)(2,1)S(1)} all-gather(bf16[2,1,1,512,192]{3,4,2,1,0:T(8,128)(2,1)S(1)} %copy.61), channel_id=1, replica_groups=mesh['chan'=32,'row'=2,'col'=8] {'row'}, dimensions={3}, use_global_device_ids=true | all-gather | bytes 1179648 | tf_op jit(solution)/shard_map/all_gather | solution.py:86
  152.4 0.9 copy.62
  153.3 3.0 %gather_fusion.2 = bf16[512,2,192]{2,1,0:T(2,128)(2,1)} fusion(bf16[2,1024,192]{2,0,1:T(2,128)(2,1)S(1)} %bitcast.101, s32[1024]{0:T(1024)S(1)} %pad_clamp_fusion), kind=kCustom, calls=%fused_computation.clone | custom fusion | bytes 788480 | tf_op jit(solution)/shard_map/jit(_take)/gather | solution.py:89
  156.3 4.2 %gather_fusion.3 = bf16[1024,2,192]{2,1,0:T(2,128)(2,1)S(1)} fusion(bf16[2,1024,192]{2,0,1:T(2,128)(2,1)S(1)} %bitcast.102, s32[1024]{0:T(1024)S(1)} %fusion.99), kind=kCustom, calls=%fused_computation.1.clone | custom fusion | bytes 1576960 | tf_op jit(solution)/shard_map/jit(_take)/gather | solution.py:95
  160.5 3.0 %gather_fusion.4 = bf16[512,2,192]{2,1,0:T(2,128)(2,1)} fusion(bf16[2,1024,192]{2,0,1:T(2,128)(2,1)S(1)} %bitcast.99, s32[1024]{0:T(1024)S(1)} %pad_clamp_fusion), kind=kCustom, calls=%fused_computation.2.clone | custom fusion | bytes 788480 | tf_op jit(solution)/shard_map/jit(_take)/gather | solution.py:89
  163.5 4.2 %gather_fusion.5 = bf16[1024,2,192]{2,1,0:T(2,128)(2,1)S(1)} fusion(bf16[2,1024,192]{2,0,1:T(2,128)(2,1)S(1)} %bitcast.100, s32[1024]{0:T(1024)S(1)} %fusion.99), kind=kCustom, calls=%fused_computation.3.clone | custom fusion | bytes 1576960 | tf_op jit(solution)/shard_map/jit(_take)/gather | solution.py:95
  167.7 1.3 copy.63
  169.0 1.3 copy.72
  170.3 0.1 broadcast_select_fusion.2
  170.5 4.2 %fusion.17 = (bf16[2,1024,192]{2,0,1:T(2,128)(2,1)S(1)}, bf16[2,1024,192]{2,0,1:T(2,128)(2,1)S(1)}) fusion(bf16[1024,2,192]{2,1,0:T(2,128)(2,1)S(1)} %gather_fusion.5, pred[1024]{0:T(1024)(128)(4,1)S(1)} %get-tuple-element.11, bf16[1024,2,192]{2,1,0:T(2,128)(2,1)S(1)} %gather_fusion.3), kind=kLoop, calls=%fused_computation.34 | loop fusion | flops 786432 | bytes 3146752 | tf_op jit(solution)/shard_map/jit(_take)/select_n | solution.py:95
  174.8 1.6 fusion.12
  176.3 4.0 %multiply_convert_fusion = bf16[2,1024,1024]{2,1,0:T(8,128)(2,1)} fusion(f32[2,1024,1024]{2,1,0:T(8,128)S(1)} %fusion.12, bf16[2,1024,192]{2,0,1:T(2,128)(2,1)S(1)} %get-tuple-element.32, bf16[2,512,192]{1,2,0:T(8,128)(2,1)S(1)} %bitcast.111, bf16[2,512,192]{1,2,0:T(8,128)(2,1)S(1)} %bitcast.104), kind=kOutput, calls=%fused_computation.6 | convolution fusion | flops 813170688 | bytes 14155776 | tf_op jit(solution)/shard_map/kpx,kqx->kpq/dot_general | solution.py:96
  (17 shorter events, 0.4 us)
Async XLA Ops:
  0.0 118.1 %copy-start = (s32[512]{0:T(512)S(1)}, s32[512]{0:T(512)}, u32[]{:S(2)}) copy-start(s32[512]{0:T(512)} %param.11) | copy-start | bytes 6148
  7.2 3.9 %copy-start.3 = (bf16[2,2,2,52736]{3,2,1,0:T(2,128)(2,1)S(1)}, bf16[2,2,2,52736]{3,2,1,0:T(2,128)(2,1)}, u32[]{:S(2)}) copy-start(bf16[2,2,2,52736]{3,2,1,0:T(2,128)(2,1)} %param.8) | copy-start | bytes 2531332
  17.4 1.6 copy-start.2
  17.7 1.3 copy-start.1
  28.0 48.0 %all-to-all-start = ((bf16[2,32,8,2,192]{4,2,3,0,1:T(8,128)(2,1)}), bf16[2,32,8,2,192]{4,2,3,0,1:T(8,128)(2,1)S(1)}, u32[]{:S(2)}, u32[]{:S(2)}) async-start(bf16[2,32,8,2,192]{4,2,3,0,1:T(8,128)(2,1)} %copy.57), calls=%async_computation | async-start | bytes 1048576 | tf_op jit(solution)/shard_map/all_to_all | solution.py:72
  76.0 35.7 %all-to-all-start.2 = ((bf16[2,32,8,2,192]{4,2,3,0,1:T(8,128)(2,1)}), bf16[2,32,8,2,192]{4,2,3,0,1:T(8,128)(2,1)S(1)}, u32[]{:S(2)}, u32[]{:S(2)}) async-start(bf16[2,32,8,2,192]{4,2,3,0,1:T(8,128)(2,1)} %copy.66), calls=%async_computation.2 | async-start | bytes 1048576 | tf_op jit(solution)/shard_map/all_to_all | solution.py:72
  111.7 14.9 %all-to-all-start.1 = ((bf16[2,1,8,64,192]{4,3,0,1,2:T(8,128)(2,1)}), bf16[2,1,8,64,192]{4,3,0,1,2:T(8,128)(2,1)S(1)}, u32[]{:S(2)}, u32[]{:S(2)}) async-start(bf16[2,1,8,64,192]{4,3,0,1,2:T(8,128)(2,1)} %copy.59), calls=%async_computation.1 | async-start | bytes 1048576 | tf_op jit(solution)/shard_map/all_to_all | solution.py:71
  126.6 14.5 %all-to-all-start.3 = ((bf16[2,1,8,64,192]{4,3,0,1,2:T(8,128)(2,1)}), bf16[2,1,8,64,192]{4,3,0,1,2:T(8,128)(2,1)S(1)}, u32[]{:S(2)}, u32[]{:S(2)}) async-start(bf16[2,1,8,64,192]{4,3,0,1,2:T(8,128)(2,1)} %copy.68), calls=%async_computation.3 | async-start | bytes 1048576 | tf_op jit(solution)/shard_map/all_to_all | solution.py:71
where the time goes:
time: 181 us; the launch traced here: 180 us
  waiting for transfers between devices  56.1 us (31%)
  local copies, waits for them, and re-layouts  44.3 us (24%)
  starting transfers between devices  34.6 us (19%)
  matrix products  19.4 us (11%)
  other arithmetic  15.6 us (9%)
  blocking collectives  10.1 us (6%)
    all_to_all x2, waiting for transfers between devices, shards(): lax.all_to_all(result.reshape(CAP, chan_count, cols_count, local_inputs,...  47.3 us
    all_to_all x2, starting transfers between devices, shards(): lax.all_to_all(result.reshape(CAP, chan_count, cols_count, local_inputs,...  22.3 us
    dot_general x2, matrix products, shards(): jnp.einsum('iasj,ajbkg->kgibs', summed, table, precision=lax.Precision.HI...  13.8 us
    all_to_all x2, starting transfers between devices, shards(): lax.all_to_all(lax.all_to_all(result.reshape(CAP, chan_count, cols_count,...  12.3 us
    all_gather x2, blocking collectives, shards(): gathered = lax.all_gather(turned, 'row', axis=3, tiled=True)  10.1 us
    all_to_all x2, waiting for transfers between devices, shards(): lax.all_to_all(lax.all_to_all(result.reshape(CAP, chan_count, cols_count,...  8.86 us
    gather x4, local copies, waits for them, and re-layouts, shards(): rows = jnp.take(flat, row_pick, axis=1)  8.64 us
    gather x2, local copies, waits for them, and re-layouts, shards(): columns = jnp.take(flat, located, axis=1)  8.34 us
  transfers between devices with their start and end apart: 4, of which 4 were waited for; matrix products, arithmetic and copies ran while one was open for 12% of the time, Pallas kernels for 0%

commit v1 on v0

--- a/solution.py
+++ b/solution.py
@@ -68,21 +68,19 @@
                 * signal[:, :, tap_index : tap_index + spec_len, :]
             )
         result = jnp.einsum("iasj,ajbkg->kgibs", summed, table, precision=lax.Precision.HIGHEST)
-        turned = lax.all_to_all(
-            lax.all_to_all(
-                result.reshape(CAP, chan_count, cols_count, local_inputs, 2 * spec_len).astype(
-                    jnp.bfloat16
-                ),
-                "chan",
-                split_axis=1,
-                concat_axis=3,
-                tiled=True,
+        x = lax.all_to_all(
+            result.reshape(CAP, chan_count, cols_count, local_inputs, 2 * spec_len).astype(
+                jnp.bfloat16
             ),
-            "col",
-            split_axis=2,
+            "chan",
+            split_axis=1,
             concat_axis=3,
             tiled=True,
         )
+        n_dev = lax.axis_size("col")
+        shards_2 = jnp.stack(jnp.split(x, n_dev, axis=2), axis=0)
+        shards_2 = lax.all_to_all(shards_2, "col", split_axis=0, concat_axis=0)
+        turned = jnp.concatenate(shards_2, axis=3)
         gathered = lax.all_gather(turned, "row", axis=3, tiled=True)
         flat = gathered.reshape(CAP, total_inputs, -1)
         width = flat.shape[2]

time: 181 us -> 170 us (0.939)
  waiting for transfers between devices: 56.1 us -> 37.3 us
  local copies, waits for them, and re-layouts: 44.3 us -> 54.8 us
    all_to_all x2, waiting for transfers between devices: 47.3 us -> 35 us  [shards(): lax.all_to_all(result.reshape(CAP, chan_count, cols_count, local_inputs,...]
    unnamed x8 -> x22, local copies, waits for them, and re-layouts: 1.33 us -> 10.2 us
    all_to_all x2, waiting for transfers between devices: 8.86 us -> 2.34 us  [shards(): shards_2 = lax.all_to_all(shards_2, 'col', split_axis=0, concat_axis=0)]
    split x0 -> x2, local copies, waits for them, and re-layouts: none -> 2.25 us  [shards(): shards_2 = jnp.stack(jnp.split(x, n_dev, axis=2), axis=0)]
    all_to_all x4 -> x2, local copies, waits for them, and re-layouts: 1.88 us -> 0.07 us  [shards(): lax.all_to_all(result.reshape(CAP, chan_count, cols_count, local_inputs,...]
  transfers between devices with their start and end apart: 4 -> 4, of which waited for: 4 -> 3; matrix products, arithmetic and copies ran while one was open for 12% -> 24% of each run, Pallas kernels for 0% -> 0%
where the time goes in v1:
time: 170 us; the launch traced here: 169 us
  local copies, waits for them, and re-layouts  54.8 us (32%)
  waiting for transfers between devices  37.3 us (22%)
  starting transfers between devices  33.1 us (19%)
  matrix products  19.2 us (11%)
  other arithmetic  15.6 us (9%)
  blocking collectives  8.96 us (5%)
    all_to_all x2, waiting for transfers between devices, shards(): lax.all_to_all(result.reshape(CAP, chan_count, cols_count, local_inputs,...  35 us
    all_to_all x2, starting transfers between devices, shards(): lax.all_to_all(result.reshape(CAP, chan_count, cols_count, local_inputs,...  22.4 us
    dot_general x2, matrix products, shards(): jnp.einsum('iasj,ajbkg->kgibs', summed, table, precision=lax.Precision.HI...  13.6 us
    all_to_all x2, starting transfers between devices, shards(): shards_2 = lax.all_to_all(shards_2, 'col', split_axis=0, concat_axis=0)  10.7 us
    unnamed x22, local copies, waits for them, and re-layouts  10.2 us
    all_gather x2, blocking collectives, shards(): gathered = lax.all_gather(turned, 'row', axis=3, tiled=True)  8.96 us
    gather x4, local copies, waits for them, and re-layouts, shards(): rows = jnp.take(flat, row_pick, axis=1)  8.63 us
    gather x2, local copies, waits for them, and re-layouts, shards(): columns = jnp.take(flat, located, axis=1)  8.34 us
  transfers between devices with their start and end apart: 4, of which 3 were waited for; matrix products, arithmetic and copies ran while one was open for 24% of the time, Pallas kernels for 0%

profile of v1, /device:TPU:1, one launch (start us, length us, event | category | flops | bytes accessed | tf_op | source)
XLA Modules:
  0.0 169.3 jit_solution(9420044969200141294)
XLA Ops:
  0.0 0.8 convert_reduce_fusion
  0.8 0.7 iota_add_fusion
  1.5 0.3 reduce-window.9
  2.1 1.0 fusion.109
  3.3 0.1 reshape.339
  3.4 3.8 %sort.17 = (s32[384]{0:T(512)}, s32[384]{0:T(512)S(1)}) sort(s32[384]{0:T(512)S(1)} %iota_add_fusion, s32[384]{0:T(512)S(1)} %iota.40), dimensions={0}, to_apply=%region_3.4 | sort | flops 3456 | bytes 6144 | tf_op jit(solution)/shard_map/jit(argsort)/sort | solution.py:16
  7.2 3.5 %gather_fusion = s32[512]{0:T(512)S(1)} fusion(s32[384]{0:T(512)S(1)} %get-tuple-element.8, s32[1024]{0:T(1024)S(1)} %pad_clamp_fusion.1), kind=kCustom, calls=%fused_computation.4 | custom fusion | bytes 6144 | tf_op jit(solution)/shard_map/jit(_take)/gather | solution.py:24
  10.7 0.1 reshape.338
  10.9 0.1 bitcast_select_fusion
  11.1 0.6 slice_convert_fusion
  11.7 1.5 reshape.304
  13.2 4.2 %fusion.71 = (f32[512,1,2,256]{3,0,2,1:T(8,128)S(1)}, f32[512,1,2,256]{3,0,2,1:T(8,128)S(1)}, f32[512,1,2,256]{3,0,2,1:T(8,128)S(1)}) fusion(f32[2,256]{1,0:T(2,128)S(1)} %compare_select_fusion.6, s32[2,256]{1,0:T(2,128)S(1)} %copy.220), kind=kLoop, calls=%fused_computation.100 | loop fusion | flops 4456448 | bytes 3149824 | tf_op jit(solution)/shard_map/neg | solution.py:45
  17.4 0.3 maximum_bitcast_fusion.3
  17.7 1.3 copy-done.1
  19.0 4.6 %fusion.7 = bf16[2,256,2,2,96]{1,4,2,0,3:T(8,128)(2,1)} fusion(f32[1,512,2,2,256]{4,1,0,3,2:T(8,128)S(1)} %get-tuple-element.14, f32[1,512,2,2,256]{4,1,0,3,2:T(8,128)S(1)} %get-tuple-element.13, f32[2,2,103,512]{3,2,1,0:T(8,128)S(1)} %copy-done.2, f32[512]{0:T(512)S(1)} %bitcast.163, f32[512]{0:T(512)S(1)} %bitcast.165, f32[512]{0:T(512)S(1)} %bitcast.153, ...), kind=kOutput, calls=%fused_computation.22 | convolution fusion | flops 2420113408 | bytes 10895360 | tf_op jit(solution)/shard_map/iasj,ajbkg->kgibs/dot_general | solution.py:70
  23.6 1.3 copy.230
  24.9 1.1 convert_element_type.73
  26.1 1.9 %copy.231 = bf16[2,32,8,2,192]{4,2,3,0,1:T(8,128)(2,1)} copy(bf16[2,32,8,2,192]{4,2,1,3,0:T(8,128)(2,1)} %convert_element_type.73) | data formatting | bytes 786432 | tf_op jit(solution)/shard_map/convert_element_type | solution.py:72
  28.0 17.0 %all-to-all-start.2 = ((bf16[2,32,8,2,192]{4,2,3,0,1:T(8,128)(2,1)}), bf16[2,32,8,2,192]{4,2,3,0,1:T(8,128)(2,1)S(1)}, u32[]{:S(2)}, u32[]{:S(2)}) async-start(bf16[2,32,8,2,192]{4,2,3,0,1:T(8,128)(2,1)} %copy.231), calls=%async_computation.2 | async-start | bytes 1048576 | tf_op jit(solution)/shard_map/all_to_all | solution.py:71
  45.0 1.5 reshape.303
  46.5 9.0 %fusion.6 = bf16[2,256,2,2,96]{1,4,2,0,3:T(8,128)(2,1)} fusion(f32[1,512,2,2,256]{4,1,0,3,2:T(8,128)} %copy-done.1, f32[1,512,2,2,256]{4,1,0,3,2:T(8,128)S(1)} %get-tuple-element.13, f32[2,2,103,512]{3,2,1,0:T(8,128)} %reshape.303, f32[512]{0:T(512)S(1)} %bitcast.164, f32[512]{0:T(512)S(1)} %bitcast.166, f32[512]{0:T(512)S(1)} %bitcast.154, ...), kind=kOutput, calls=%fused_computation.21 | convolution fusion | flops 2420113408 | bytes 10895360 | tf_op jit(solution)/shard_map/iasj,ajbkg->kgibs/dot_general | solution.py:70
  55.5 1.3 copy.222
  56.8 0.3 convert_element_type.68
  57.2 0.9 copy.223
  58.1 6.9 %gather_fusion.1 = s32[1024]{0:T(1024)S(1)} fusion(s32[512]{0:T(512)S(1)} %copy-done, s32[1024]{0:T(1024)S(1)} %broadcast_clamp_fusion), kind=kCustom, calls=%fused_computation.5 | custom fusion | bytes 12288 | tf_op jit(solution)/shard_map/jit(_take)/gather | solution.py:49
  65.1 10.8 %all-to-all-done.2 = bf16[2,32,8,2,192]{4,2,3,0,1:T(8,128)(2,1)S(1)} async-done(((bf16[2,32,8,2,192]{4,2,3,0,1:T(8,128)(2,1)}), bf16[2,32,8,2,192]{4,2,3,0,1:T(8,128)(2,1)S(1)}, u32[]{:S(2)}, u32[]{:S(2)}) %all-to-all-start.2) | async-done | bytes 393248 | tf_op jit(solution)/shard_map/all_to_all | solution.py:71
  75.9 5.3 %all-to-all-start = ((bf16[2,32,8,2,192]{4,2,3,0,1:T(8,128)(2,1)}), bf16[2,32,8,2,192]{4,2,3,0,1:T(8,128)(2,1)S(1)}, u32[]{:S(2)}, u32[]{:S(2)}) async-start(bf16[2,32,8,2,192]{4,2,3,0,1:T(8,128)(2,1)} %copy.223), calls=%async_computation | async-start | bytes 1048576 | tf_op jit(solution)/shard_map/all_to_all | solution.py:71
  81.3 1.1 fusion.105
  82.4 0.6 bitcast_dynamic-update-slice_fusion.7
  83.1 0.6 bitcast_dynamic-update-slice_fusion.6
  83.7 0.6 bitcast_dynamic-update-slice_fusion.5
  84.3 0.6 bitcast_dynamic-update-slice_fusion.4
  85.0 0.6 bitcast_dynamic-update-slice_fusion.3
  85.6 0.6 bitcast_dynamic-update-slice_fusion.2
  86.2 0.6 bitcast_dynamic-update-slice_fusion.1
  86.9 0.6 bitcast_dynamic-update-slice_fusion
  87.5 24.2 %all-to-all-done = bf16[2,32,8,2,192]{4,2,3,0,1:T(8,128)(2,1)S(1)} async-done(((bf16[2,32,8,2,192]{4,2,3,0,1:T(8,128)(2,1)}), bf16[2,32,8,2,192]{4,2,3,0,1:T(8,128)(2,1)S(1)}, u32[]{:S(2)}, u32[]{:S(2)}) %all-to-all-start) | async-done | bytes 393248 | tf_op jit(solution)/shard_map/all_to_all | solution.py:71
  111.7 6.4 %all-to-all-start.3 = ((bf16[8,2,1,1,64,192]{5,4,1,3,2,0:T(8,128)(2,1)}), bf16[8,2,1,1,64,192]{5,4,1,3,2,0:T(8,128)(2,1)S(1)}, u32[]{:S(2)}, u32[]{:S(2)}) async-start(bf16[8,2,1,1,64,192]{5,4,1,3,2,0:T(8,128)(2,1)} %bitcast_dynamic-update-slice_fusion), calls=%async_computation.3 | async-start | bytes 1048576 | tf_op jit(solution)/shard_map/all_to_all | solution.py:82
  118.1 1.1 fusion.106
  119.2 0.6 bitcast_dynamic-update-slice_fusion.15
  119.8 0.6 bitcast_dynamic-update-slice_fusion.14
  120.5 0.6 bitcast_dynamic-update-slice_fusion.13
  121.1 0.6 bitcast_dynamic-update-slice_fusion.12
  121.7 0.6 bitcast_dynamic-update-slice_fusion.11
  122.4 0.6 bitcast_dynamic-update-slice_fusion.10
  123.0 0.6 bitcast_dynamic-update-slice_fusion.9
  123.6 0.6 bitcast_dynamic-update-slice_fusion.8
  124.3 2.3 %all-to-all-done.3 = bf16[8,2,1,1,64,192]{5,4,1,3,2,0:T(8,128)(2,1)S(1)} async-done(((bf16[8,2,1,1,64,192]{5,4,1,3,2,0:T(8,128)(2,1)}), bf16[8,2,1,1,64,192]{5,4,1,3,2,0:T(8,128)(2,1)S(1)}, u32[]{:S(2)}, u32[]{:S(2)}) %all-to-all-start.3) | async-done | bytes 393248 | tf_op jit(solution)/shard_map/all_to_all | solution.py:82
  126.6 4.3 %all-to-all-start.1 = ((bf16[8,2,1,1,64,192]{5,4,1,3,2,0:T(8,128)(2,1)}), bf16[8,2,1,1,64,192]{5,4,1,3,2,0:T(8,128)(2,1)S(1)}, u32[]{:S(2)}, u32[]{:S(2)}) async-start(bf16[8,2,1,1,64,192]{5,4,1,3,2,0:T(8,128)(2,1)} %bitcast_dynamic-update-slice_fusion.8), calls=%async_computation.1 | async-start | bytes 1048576 | tf_op jit(solution)/shard_map/all_to_all | solution.py:82
  131.0 0.2 copy.234
  131.2 6.4 %all_gather.7 = bf16[2,1,1,1024,192]{3,4,2,1,0:T(8,128)(2,1)S(1)} all-gather(bf16[2,1,1,512,192]{3,4,2,1,0:T(8,128)(2,1)S(1)} %copy.234), channel_id=1, replica_groups=mesh['chan'=32,'row'=2,'col'=8] {'row'}, dimensions={3}, use_global_device_ids=true | all-gather | bytes 1179648 | tf_op jit(solution)/shard_map/all_gather | solution.py:84
  137.5 0.9 copy.235
  138.4 3.0 %gather_fusion.4 = bf16[512,2,192]{2,1,0:T(2,128)(2,1)} fusion(bf16[2,1024,192]{2,0,1:T(2,128)(2,1)S(1)} %bitcast.135, s32[1024]{0:T(1024)S(1)} %get-tuple-element.52), kind=kCustom, calls=%fused_computation.2.clone | custom fusion | bytes 788480 | tf_op jit(solution)/shard_map/jit(_take)/gather | solution.py:87
  141.5 4.2 %gather_fusion.5 = bf16[1024,2,192]{2,1,0:T(2,128)(2,1)S(1)} fusion(bf16[2,1024,192]{2,0,1:T(2,128)(2,1)S(1)} %bitcast.136, s32[1024]{0:T(1024)S(1)} %get-tuple-element.53), kind=kCustom, calls=%fused_computation.3.clone | custom fusion | bytes 1576960 | tf_op jit(solution)/shard_map/jit(_take)/gather | solution.py:93
  145.7 0.2 copy.226
  145.9 2.6 %all_gather.6 = bf16[2,1,1,1024,192]{3,4,2,1,0:T(8,128)(2,1)S(1)} all-gather(bf16[2,1,1,512,192]{3,4,2,1,0:T(8,128)(2,1)S(1)} %copy.226), channel_id=1, replica_groups=mesh['chan'=32,'row'=2,'col'=8] {'row'}, dimensions={3}, use_global_device_ids=true | all-gather | bytes 1179648 | tf_op jit(solution)/shard_map/all_gather | solution.py:84
  148.5 0.9 copy.227
  149.4 3.0 %gather_fusion.2 = bf16[512,2,192]{2,1,0:T(2,128)(2,1)} fusion(bf16[2,1024,192]{2,0,1:T(2,128)(2,1)S(1)} %bitcast.133, s32[1024]{0:T(1024)S(1)} %get-tuple-element.52), kind=kCustom, calls=%fused_computation.clone | custom fusion | bytes 788480 | tf_op jit(solution)/shard_map/jit(_take)/gather | solution.py:87
  152.4 4.2 %gather_fusion.3 = bf16[1024,2,192]{2,1,0:T(2,128)(2,1)S(1)} fusion(bf16[2,1024,192]{2,0,1:T(2,128)(2,1)S(1)} %bitcast.134, s32[1024]{0:T(1024)S(1)} %get-tuple-element.53), kind=kCustom, calls=%fused_computation.1.clone | custom fusion | bytes 1576960 | tf_op jit(solution)/shard_map/jit(_take)/gather | solution.py:93
  156.6 1.3 copy.236
  157.9 1.3 copy.228
  159.4 4.2 %fusion.17 = (bf16[2,1024,192]{2,0,1:T(2,128)(2,1)S(1)}, bf16[2,1024,192]{2,0,1:T(2,128)(2,1)S(1)}) fusion(bf16[1024,2,192]{2,1,0:T(2,128)(2,1)S(1)} %gather_fusion.5, pred[1024]{0:T(1024)(128)(4,1)S(1)} %get-tuple-element.11, bf16[1024,2,192]{2,1,0:T(2,128)(2,1)S(1)} %gather_fusion.3), kind=kLoop, calls=%fused_computation.34 | loop fusion | flops 786432 | bytes 3146752 | tf_op jit(solution)/shard_map/jit(_take)/select_n | solution.py:93
  163.7 1.6 fusion.12
  165.2 4.0 %multiply_convert_fusion = bf16[2,1024,1024]{2,1,0:T(8,128)(2,1)} fusion(f32[2,1024,1024]{2,1,0:T(8,128)S(1)} %fusion.12, bf16[2,1024,192]{2,0,1:T(2,128)(2,1)S(1)} %get-tuple-element.48, bf16[2,512,192]{1,2,0:T(8,128)(2,1)S(1)} %bitcast.147, bf16[2,512,192]{1,2,0:T(8,128)(2,1)S(1)} %bitcast.140), kind=kOutput, calls=%fused_computation.6 | convolution fusion | flops 813170688 | bytes 14155776 | tf_op jit(solution)/shard_map/kpx,kqx->kpq/dot_general | solution.py:94
  (31 shorter events, 1.0 us)
Async XLA Ops:
  0.0 58.1 %copy-start = (s32[512]{0:T(512)S(1)}, s32[512]{0:T(512)}, u32[]{:S(2)}) copy-start(s32[512]{0:T(512)} %param.11) | copy-start | bytes 6148
  7.2 3.9 %copy-start.3 = (bf16[2,2,2,52736]{3,2,1,0:T(2,128)(2,1)S(1)}, bf16[2,2,2,52736]{3,2,1,0:T(2,128)(2,1)}, u32[]{:S(2)}) copy-start(bf16[2,2,2,52736]{3,2,1,0:T(2,128)(2,1)} %param.8) | copy-start | bytes 2531332
  17.4 1.6 copy-start.2
  17.7 1.3 copy-start.1
  28.0 47.9 %all-to-all-start.2 = ((bf16[2,32,8,2,192]{4,2,3,0,1:T(8,128)(2,1)}), bf16[2,32,8,2,192]{4,2,3,0,1:T(8,128)(2,1)S(1)}, u32[]{:S(2)}, u32[]{:S(2)}) async-start(bf16[2,32,8,2,192]{4,2,3,0,1:T(8,128)(2,1)} %copy.231), calls=%async_computation.2 | async-start | bytes 1048576 | tf_op jit(solution)/shard_map/all_to_all | solution.py:71
  75.9 35.8 %all-to-all-start = ((bf16[2,32,8,2,192]{4,2,3,0,1:T(8,128)(2,1)}), bf16[2,32,8,2,192]{4,2,3,0,1:T(8,128)(2,1)S(1)}, u32[]{:S(2)}, u32[]{:S(2)}) async-start(bf16[2,32,8,2,192]{4,2,3,0,1:T(8,128)(2,1)} %copy.223), calls=%async_computation | async-start | bytes 1048576 | tf_op jit(solution)/shard_map/all_to_all | solution.py:71
  111.7 14.9 %all-to-all-start.3 = ((bf16[8,2,1,1,64,192]{5,4,1,3,2,0:T(8,128)(2,1)}), bf16[8,2,1,1,64,192]{5,4,1,3,2,0:T(8,128)(2,1)S(1)}, u32[]{:S(2)}, u32[]{:S(2)}) async-start(bf16[8,2,1,1,64,192]{5,4,1,3,2,0:T(8,128)(2,1)} %bitcast_dynamic-update-slice_fusion), calls=%async_computation.3 | async-start | bytes 1048576 | tf_op jit(solution)/shard_map/all_to_all | solution.py:82
  126.6 19.0 %all-to-all-start.1 = ((bf16[8,2,1,1,64,192]{5,4,1,3,2,0:T(8,128)(2,1)}), bf16[8,2,1,1,64,192]{5,4,1,3,2,0:T(8,128)(2,1)S(1)}, u32[]{:S(2)}, u32[]{:S(2)}) async-start(bf16[8,2,1,1,64,192]{5,4,1,3,2,0:T(8,128)(2,1)} %bitcast_dynamic-update-slice_fusion.8), calls=%async_computation.1 | async-start | bytes 1048576 | tf_op jit(solution)/shard_map/all_to_all | solution.py:82
